TPU v7x, 128 devices: a whole 4x4x4 slice. The times are simulated.
128 devices in a mesh: grp: 8 (over x, z_lo), slab: 16 (over z_hi, y, core).
Axes of the slice: x: 4, y: 4, z: 4 (z_hi: 2, z_lo: 2; z = z_hi * 2 + z_lo), core: 2. Of those that a mesh axis runs over, the one named last changes fastest.
Arguments:
- valence_waves: bfloat16 [8, 128, 128, 256], P('grp', 'slab'), may hold values from -6 to 6
- conduction_waves: bfloat16 [128, 128, 128, 256], P('grp', 'slab'), may hold values from -6 to 6
- valence_energy: float32 [8], replicated, may hold values from -3 to -0.5
- conduction_energy: float32 [128], P('grp'), may hold values from 0.5 to 4
- occupation: int32 [8], replicated, may hold values from 1 to 2
- gvec_ids: int32 [12000], replicated, may hold values from 0 to 32767, as said below
Outputs:
- chi0: float32 [2, 12000, 12000], P(None, 'grp', 'slab')
Inputs may be any that keep to these rules, and one draw needn't show every extreme that they name: `gvec_ids`: 12000 distinct indices (kx 32 + ky) * 32 + kz of points of the frequency box, ordered by their distance from a shifted centre; every one has f(ky)^2 + f(kz)^2 <= 196.
All inputs are finite; a program needn't handle non-finite values.
Results may differ from a plain program's by a relative error of at most 0.0086.
Values may be sent and summed in bfloat16 or wider, within the bound.
A program may use at most 256 MiB of HBM per device.

v0:
```python
import functools
import math

import jax
import jax.numpy as jnp
import ml_dtypes
import numpy as np
from jax import lax
from jax.experimental import pallas as pl
from jax.experimental.pallas import tpu as pltpu
from jax.sharding import PartitionSpec as P

NV = 8
NC = 128
NF = 128
KB = 32
NG = 12000
NGRP = 8
NSLAB = 16
NX = NF // NSLAB
HX = NX // 2
NR = 24
RB = NG // NGRP
CB = NG // NSLAB
RP = 1536
CP = 768
NBOX = NR * KB
MESH = pl.DeviceIdType.MESH
BF = jnp.bfloat16
F32 = jnp.float32

WIDE = [9, -9, 11, -11, 5, -5]
NARROW = [13, -13, 12, -12, 14, -14]
SINGLE = [0, 1, -1, 2, -2, 3, -3, 4, -4, 6, -6, 7, -7, 8, -8, 10, -10]
ROW_FREQ = SINGLE[:16] + [SINGLE[16]] + WIDE + [15] + [15] + NARROW + [15]


def freq(j):
    return j - KB if j >= KB // 2 else j


def row_tables():
    row = np.zeros(KB, np.int32)
    shifted = np.zeros(KB, np.int32)
    for place, f in enumerate(ROW_FREQ[:NR]):
        if f != 15:
            row[f % KB] = place
    for place, f in enumerate(NARROW):
        row[f % KB] = 17 + place
        shifted[f % KB] = KB // 2
    return row, shifted


def phases(positions, freqs):
    angle = np.mod(np.outer(positions, freqs), NF).astype(np.float32) * np.float32(2.0 * math.pi / NF)
    return np.cos(angle).astype(np.float32), np.sin(angle).astype(np.float32)


def depth_weights():
    cos, sin = phases(np.arange(NF), [freq(j) for j in range(KB)])
    w = np.zeros((4, 2, NF, 2, KB, 4), np.float32)
    for vl in range(4):
        w[vl, 0, :, 0, :, vl] = cos
        w[vl, 1, :, 0, :, vl] = sin
        w[vl, 0, :, 1, :, vl] = -sin
        w[vl, 1, :, 1, :, vl] = cos
    return w.reshape(8 * NF, 8 * KB).astype(ml_dtypes.bfloat16)


def height_weights():
    cos, sin = phases(np.arange(NF), ROW_FREQ)
    return np.concatenate([cos.T, sin.T], 0).astype(ml_dtypes.bfloat16)


def wide_mask():
    mask = np.ones((8, KB, 4), np.float32)
    for place, f in enumerate(WIDE):
        half = math.isqrt(196 - f * f)
        for j in range(KB):
            if abs(freq(j)) > half:
                mask[1 + place, j] = 0.0
    return mask.reshape(8, 4 * KB)


def box_weights():
    cos, sin = phases(np.arange(NF), [freq(j) for j in range(KB)])
    cos = cos.T.reshape(KB, NSLAB, 2, HX).transpose(0, 2, 1, 3)
    sin = sin.T.reshape(KB, NSLAB, 2, HX).transpose(0, 2, 1, 3)
    t = np.zeros((2, KB, 2, NSLAB, 2, HX), np.float32)
    t[0, :, :, :, 0] = cos
    t[0, :, :, :, 1] = sin
    t[1, :, :, :, 0] = -sin
    t[1, :, :, :, 1] = cos
    high = t.astype(ml_dtypes.bfloat16)
    low = (t - high.astype(np.float32)).astype(ml_dtypes.bfloat16)
    pair = np.zeros((2, 2, 2, KB, 2, NSLAB, 2, 2, HX), ml_dtypes.bfloat16)
    for r in range(2):
        pair[r, 0, :, :, :, :, r] = high
        pair[r, 1, :, :, :, :, r] = low
    return pair.reshape(8 * KB, 4 * NF)


def lane_order():
    m = np.zeros((2, 2, KB, 4, KB, 2, 2, 4), np.float32)
    for reim in range(2):
        for vg in range(2):
            for kz in range(KB):
                for vl in range(4):
                    m[reim, vg, kz, vl, kz, reim, vg, vl] = 1.0
    return m.reshape(512, 512).astype(ml_dtypes.bfloat16)


def place_in_groups():
    g = lax.axis_index("grp")
    gx, gz = g // 2, lax.rem(g, 2)

    def at(dx, dz):
        return lax.rem(gx + dx + 4, 4) * 2 + (lax.rem(gz + dz, 2))

    return g, at


def place_in_slabs():
    s = lax.axis_index("slab")
    sz, sy, sc = s // 8, lax.rem(s // 2, 4), lax.rem(s, 2)

    def at(dy, dz, dc):
        return lax.rem(sz + dz, 2) * 8 + lax.rem(sy + dy + 4, 4) * 2 + lax.rem(sc + dc, 2)

    return s, at


def enter(groups, slabs):
    barrier = pltpu.get_barrier_semaphore()
    for one in groups:
        pl.semaphore_signal(barrier, inc=1, device_id={"grp": one}, device_id_type=MESH)
    for one in slabs:
        pl.semaphore_signal(barrier, inc=1, device_id={"slab": one}, device_id_type=MESH)
    pl.semaphore_wait(barrier, len(groups) + len(slabs))


def remote(src, dst, send, recv, device):
    return pltpu.make_async_remote_copy(
        src_ref=src, dst_ref=dst, send_sem=send, recv_sem=recv, device_id=device, device_id_type=MESH
    )


def planes_kernel(
    val_ref, con_ref, wz_ref, ty_ref, mask_ref, out_ref, val, con, msg, wz, even, odd, first_even, first_odd, scr, con_sem, own_sem, wz_sem, vs, vr, ms, mr, local_sem
):
    g, gat = place_in_groups()
    s, sat = place_in_slabs()
    own = pltpu.make_async_copy(val_ref.at[0], val.at[0], own_sem)
    own.start()
    weights = pltpu.make_async_copy(wz_ref, wz, wz_sem)
    weights.start()

    def band(i):
        k = lax.rem(i + 16, 16) // 2
        step = lax.rem(k + 1, 4)
        step = step + lax.rem(s, 2) * (4 - 2 * step)
        return sat(lax.rem(step, 4), lax.rem(i + 17, 2), 1 - k // 4)

    def con_copy(c):
        return pltpu.make_async_copy(con_ref.at[c], con.at[c], con_sem.at[c])

    def start_con(i, _):
        con_copy(band(i)).start()
        return 0

    lax.fori_loop(0, NSLAB, start_con, 0)
    partner, ahead, behind = gat(0, 1), gat(1, 0), gat(-1, 0)
    enter([partner, ahead, behind], [lax.rem(s + i, NSLAB) for i in range(1, NSLAB)])
    own.wait()

    def hop(k, slot, to, landing):
        return [
            remote(
                val.at[slot, pl.ds(half * HX, HX)],
                val.at[landing, pl.ds(half * HX, HX)],
                vs.at[k, half],
                vr.at[landing, half],
                {"grp": to},
            )
            for half in range(2)
        ]

    to_partner, to_ahead, to_behind = hop(0, 0, partner, 1), hop(1, 0, ahead, 2), hop(2, 0, behind, 3)
    p_ahead, p_behind = hop(3, 1, ahead, 4), hop(4, 1, behind, 5)
    l_ahead, r_behind = hop(5, 2, ahead, 6), hop(6, 5, behind, 7)
    for half in range(2):
        to_ahead[half].start()
        to_behind[half].start()
        to_partner[half].start()
    weights.wait()

    def message(vg, half, c):
        return remote(
            msg.at[vg, half, c], out_ref.at[vg, half, s], ms.at[vg, half, c], mr.at[vg, half, s], {"slab": c}
        )

    def arrival(vg, half, src):
        return remote(
            msg.at[vg, half, src],
            out_ref.at[vg, half, src],
            ms.at[vg, half, src],
            mr.at[vg, half, src],
            {"slab": src},
        )

    def kept(vg, half):
        return pltpu.make_async_copy(msg.at[vg, half, s], out_ref.at[vg, half, s], local_sem.at[vg, half])

    def density(vg, half, c, buf, x):
        for y0 in range(0, NF, 32):
            rows = pl.ds(y0, 32)
            put = pl.ds(x * NF + y0, 32)
            cr = con[c, half * HX + x, rows, 0:NF]
            ci = con[c, half * HX + x, rows, NF : 2 * NF]
            for vl in range(4):
                pr = val[vg * 4 + vl, half * HX + x, rows, 0:NF]
                pi = val[vg * 4 + vl, half * HX + x, rows, NF : 2 * NF]
                buf[put, vl * 256 : vl * 256 + NF] = pr * cr + pi * ci
                buf[put, vl * 256 + NF : vl * 256 + 256] = pr * ci - pi * cr

    def along_z(part, buf, first):
        rows = pl.ds(part * HX * NF // 2, HX * NF // 2)
        first[rows, :] = jnp.dot(buf[rows, :], wz[...], preferred_element_type=F32).astype(BF)

    def along_y(x, first):
        o = jnp.dot(ty_ref[...], first[x * NF : x * NF + NF, :], preferred_element_type=F32)
        keep = mask_ref[...] > 0.5
        for reim in range(2):
            if reim == 0:
                full = o[0:32, 0:128] + o[32:64, 128:256]
            else:
                full = o[0:32, 128:256] - o[32:64, 0:128]
            merged = jnp.where(keep, full[16:24], pltpu.roll(full[24:32], 64, 1))
            base = (reim * HX + x) * NR
            scr[base : base + 16, :] = full[0:16]
            scr[base + 16 : base + 24, :] = merged

    def pack(vg, half, c):
        for r in range(0, NR, 2):
            both = jnp.concatenate(
                [scr[pl.ds(r, 2 * HX, stride=NR), :], scr[pl.ds(r + 1, 2 * HX, stride=NR), :]], 0
            )
            msg[vg, half, c, r // 2] = both.astype(BF)

    def one_band(vg, half, before, after, buf, other, first, last):
        along_z(0, buf, first)
        density(vg, half, after, other, 0)
        density(vg, half, after, other, 1)
        along_y(0, last)
        along_y(1, last)
        along_z(1, buf, first)
        density(vg, half, after, other, 2)
        density(vg, half, after, other, 3)
        along_y(2, last)
        along_y(3, last)
        pack(vg, half, before)

    for phase in range(4):
        vg, half = phase // 2, phase % 2
        if phase == 0:
            for copies in (to_partner, to_ahead, to_behind):
                copies[0].wait_recv()
            p_behind[0].start()
            p_ahead[0].start()
            l_ahead[0].start()
        if phase == 1:
            for copies in (to_partner, to_ahead, to_behind):
                copies[1].wait_recv()
            p_ahead[1].start()
            p_behind[0].wait_recv()
            r_behind[0].start()
            p_behind[1].start()
            l_ahead[1].start()
        if phase >= 2:
            for copies in (p_ahead, l_ahead, r_behind):
                copies[half].wait_recv()
        start = band(0)
        if phase == 0:
            con_copy(start).wait()
        for x in range(HX):
            density(vg, half, start, even, x)

        def two_bands(j, _):
            before, c0, c1, c2 = band(2 * j - 1), band(2 * j), band(2 * j + 1), band(2 * j + 2)
            if phase == 0:
                con_copy(c1).wait()

                @pl.when(j < NSLAB // 2 - 1)
                def _():
                    con_copy(c2).wait()

            if phase == 2:

                @pl.when(j == 2)
                def _():
                    p_behind[1].wait_recv()
                    r_behind[1].start()

            one_band(vg, half, before, c1, even, odd, first_even, first_odd)

            @pl.when(j > 0)
            def _():
                message(vg, half, before).start()

            one_band(vg, half, c0, c2, odd, even, first_odd, first_even)
            message(vg, half, c0).start()
            return 0

        lax.fori_loop(0, NSLAB // 2, two_bands, 0)
        for x in range(HX):
            along_y(x, first_odd)
        pack(vg, half, s)
        kept(vg, half).start()

    def finish(i, _):
        other = lax.rem(s + i + 1, NSLAB)
        for vg in range(2):
            for half in range(2):
                arrival(vg, half, other).wait_recv()
                message(vg, half, other).wait_send()
        return 0

    lax.fori_loop(0, NSLAB - 1, finish, 0)
    for vg in range(2):
        for half in range(2):
            kept(vg, half).wait()
    for copies in (to_partner, to_ahead, to_behind, p_ahead, p_behind, l_ahead, r_behind):
        for half in range(2):
            copies[half].wait_send()


def planes_call(valence, conduction):
    anywhere = pl.BlockSpec(memory_space=pl.ANY)
    vmem = pl.BlockSpec(memory_space=pltpu.VMEM)
    return pl.pallas_call(
        planes_kernel,
        name="planes",
        out_shape=jax.ShapeDtypeStruct((2, 2, NSLAB, NR // 2, 16, 128), BF),
        in_specs=[anywhere, anywhere, anywhere, vmem, vmem],
        out_specs=vmem,
        scratch_shapes=[
            pltpu.VMEM((8, NX, NF, 2 * NF), BF),
            pltpu.VMEM((NSLAB, NX, NF, 2 * NF), BF),
            pltpu.VMEM((2, 2, NSLAB, NR // 2, 16, 128), BF),
            pltpu.VMEM((8 * NF, 2 * NF), BF),
            pltpu.VMEM((HX * NF, 8 * NF), BF),
            pltpu.VMEM((HX * NF, 8 * NF), BF),
            pltpu.VMEM((HX * NF, 2 * NF), BF),
            pltpu.VMEM((HX * NF, 2 * NF), BF),
            pltpu.VMEM((2 * HX * NR, 128), F32),
            pltpu.SemaphoreType.DMA((NSLAB,)),
            pltpu.SemaphoreType.DMA,
            pltpu.SemaphoreType.DMA,
            pltpu.SemaphoreType.DMA((7, 2)),
            pltpu.SemaphoreType.DMA((8, 2)),
            pltpu.SemaphoreType.DMA((2, 2, NSLAB)),
            pltpu.SemaphoreType.DMA((2, 2, NSLAB)),
            pltpu.SemaphoreType.DMA((2, 2)),
        ],
        compiler_params=pltpu.CompilerParams(
            collective_id=0, has_side_effects=True, vmem_limit_bytes=56 * 1024 * 1024
        ),
    )(
        valence,
        conduction,
        jnp.asarray(depth_weights()),
        jnp.asarray(height_weights()),
        jnp.asarray(wide_mask()),
    )


def panels_kernel(
    idx_ref, in_ref, tab_ref, order_ref, fac_ref, rp_ref, cab_ref,
    xb, wide, box, blk, rows, cols, landed, cp,
    rsa, rra, csa, cra, rs, rr, cs, cr, sib_s, sib_r, lsem,
):
    g, gat = place_in_groups()
    s, sat = place_in_slabs()
    gx, gz = g // 2, lax.rem(g, 2)
    sz, yc = s // 8, lax.rem(s, 8)
    scaling = 0.5 / float(NF) ** 1.5

    barrier = pltpu.get_barrier_semaphore()
    for i in range(2 * NSLAB):
        if i:
            to = {"grp": gat(0, i // NSLAB), "slab": lax.rem(s + i, NSLAB)}
            pl.semaphore_signal(barrier, inc=1, device_id=to, device_id_type=MESH)
    for i in range(4, 16):
        to = {"grp": gat(i // 4, i // 2 % 2), "slab": sat(0, i % 2, 0)}
        pl.semaphore_signal(barrier, inc=1, device_id=to, device_id_type=MESH)

    def four_rows(j, _):
        for k in range(2):
            p = j * 2 + k
            a = [in_ref[vg, :, :, pl.ds(p, 1)].reshape(4 * NF, 128) for vg in range(2)]
            both = jnp.dot(tab_ref[...], jnp.concatenate(a, 1), preferred_element_type=F32)
            for r in range(2):
                o = both[r * 128 : r * 128 + 128]
                o = ((o[0:64] + o[64:128]) * scaling).astype(BF)
                put = pl.ds(pl.multiple_of((p * 2 + r) * KB, KB), KB)
                xb[put, 0:256] = o[0:32]
                xb[put, 256:512] = o[32:64]
        return 0

    lax.fori_loop(0, NR // 4, four_rows, 0)
    wide[...] = jnp.dot(xb[...], order_ref[...], preferred_element_type=F32)

    def spread(j, _):
        base = pl.multiple_of(j * 96, 32)
        for kz in range(KB):
            part = wide[pl.ds(base, 96), (kz // 8) * 128 : (kz // 8 + 1) * 128]
            if kz % 8:
                part = pltpu.roll(part, 128 - 16 * (kz % 8), 1)
            box[pl.ds(pl.multiple_of(kz * NBOX + base, 8), 96), :] = part
        return 0

    lax.fori_loop(0, NBOX // 96, spread, 0)
    blk[1496:1536, :] = jnp.zeros((40, 128), F32)
    pl.semaphore_wait(barrier, 43)

    lane = lax.broadcasted_iota(jnp.int32, (16, 128), 1)
    row = lax.broadcasted_iota(jnp.int32, (16, 128), 0)
    unit = jnp.where(lane == row, 1.0, 0.0).astype(BF)
    contract = (((1,), (1,)), ((), ()))

    def row_copy(b, z):
        to = {"grp": b, "slab": z * 8 + yc}
        return remote(rows.at[b], landed.at[sz, g], rsa.at[b, z], rra.at[sz, g], to)

    def row_in(b, z):
        to = {"grp": b, "slab": z * 8 + yc}
        return remote(rows.at[b], landed.at[z, b], rsa.at[b, z], rra.at[z, b], to)

    def row_keep():
        return pltpu.make_async_copy(rows.at[g], landed.at[sz, g], lsem.at[0])

    def col_copy(t, z):
        to = {"grp": gx * 2 + z, "slab": t}
        return remote(cols.at[t], cp.at[gx, gz, s], csa.at[t, z], cra.at[gz, s], to)

    def col_in(t, z):
        to = {"grp": gx * 2 + z, "slab": t}
        return remote(cols.at[t], cp.at[gx, z, t], csa.at[t, z], cra.at[z, t], to)

    def col_keep():
        return pltpu.make_async_copy(cols.at[s], cp.at[gx, gz, s], lsem.at[1])

    def one_block(i, _):
        b = lax.rem(g + yc // 2 + sz * 4 + i, NGRP)

        def pick(j, _):
            base = j * 60
            for k in range(60):
                blk[pl.ds(base + k, 1), :] = box[pl.ds(idx_ref[b * RB + base + k], 1), :]
            return 0

        lax.fori_loop(0, RB // 60, pick, 0)
        o = lax.dot_general(unit, blk[0:RP, :].astype(BF), contract, preferred_element_type=F32)
        rows[b] = (o * fac_ref[:, 0:1]).astype(BF)
        for half in range(2):
            part = blk[half * CB : half * CB + CP, :].astype(BF)
            cols[2 * b + half] = lax.dot_general(unit, part, contract, preferred_element_type=F32).astype(BF)
        for z in range(2):
            mine = jnp.logical_and(b == g, z == sz)

            @pl.when(mine)
            def _():
                row_keep().start()

            @pl.when(jnp.logical_not(mine))
            def _():
                row_copy(b, z).start()

            for half in range(2):
                own = jnp.logical_and(2 * b + half == s, z == gz)

                @pl.when(own)
                def _():
                    col_keep().start()

                @pl.when(jnp.logical_not(own))
                def _():
                    col_copy(2 * b + half, z).start()

        return 0

    lax.fori_loop(0, NGRP, one_block, 0)

    def over_rows(act):
        def step(i, _):
            b, z = i // 2, lax.rem(i, 2)

            @pl.when(jnp.logical_not(jnp.logical_and(b == g, z == sz)))
            def _():
                act(b, z)

            return 0

        lax.fori_loop(0, 2 * NGRP, step, 0)

    def over_cols(act):
        def step(i, _):
            t, z = i // 2, lax.rem(i, 2)

            @pl.when(jnp.logical_not(jnp.logical_and(t == s, z == gz)))
            def _():
                act(t, z)

            return 0

        lax.fori_loop(0, 2 * NSLAB, step, 0)

    def row_part(dy, dc, half):
        return rp_ref.at[sat(dy, 0, dc) % 8, pl.ds(half * 768, 768)]

    def row_hop(k, dy, half, to, land):
        part = row_part(dy, 0, half)
        return remote(part, part, rs.at[k], rr.at[land], {"slab": sat(to, 0, 0)})

    def row_wait(land, dy, half):
        part = row_part(dy, 0, half)
        remote(part, part, rs.at[0], rr.at[land], {"slab": sat(1, 0, 0)}).wait_recv()

    def side(k, dy, half, dc=0):
        part = row_part(dy, dc, half)
        return remote(part, part, sib_s.at[k], sib_r.at[k], {"slab": sat(0, 0, 1)})

    def col_part(dx, half):
        return cp.at[gat(dx, 0) // 2, half]

    def col_hop(k, dx, half, to, land):
        part = col_part(dx, half)
        return remote(part, part, cs.at[k], cr.at[land], {"grp": gat(to, 0)})

    def col_wait(land, dx, half):
        part = col_part(dx, half)
        remote(part, part, cs.at[0], cr.at[land], {"grp": gat(1, 0)}).wait_recv()

    hops = [(0, 0, 1, 0), (0, 1, -1, 3), (0, 1, 1, 1), (0, 0, -1, 2), (-1, 0, 1, 4), (1, 1, -1, 5)]
    arrivals = [(0, -1, 0), (3, 1, 1), (1, -1, 1), (2, 1, 0), (4, 2, 0), (5, 2, 1)]
    row_hops = [row_hop(k, *hop) for k, hop in enumerate(hops)]
    col_hops = [col_hop(k, *hop) for k, hop in enumerate(hops)]
    sides = [side(0, 0, 0), side(1, 0, 1)] + [side(2 + k, dy, half) for k, (_, dy, half) in enumerate(arrivals)]

    def arrange(dx, half):
        x = gat(dx, 0) // 2

        def step(t, _):
            part = cp[x, half, pl.ds(t, 1)].reshape(16, CP)
            put = pl.multiple_of(lax.rem(t, 8) * 256 + (t // 8) * 128 + x * 32 + half * 16, 16)
            cab_ref[pl.ds(put, 16), 0:CP] = part
            value = part.astype(F32)
            cab_ref[pl.ds(put, 16), CP : 2 * CP] = jnp.concatenate([-value[8:16], value[0:8]], 0).astype(BF)
            return 0

        lax.fori_loop(0, NSLAB, step, 0)

    row_keep().wait()
    over_rows(lambda b, z: row_in(b, z).wait_recv())
    for j in range(RP // 128):
        part = landed[:, :, :, j * 128 : (j + 1) * 128].reshape(256, 128).astype(F32)
        rp_ref[yc, j * 128 : (j + 1) * 128, :] = part.T.astype(BF)
        if j == 5:
            row_hops[0].start()
            sides[0].start()
    row_hops[1].start()
    row_hops[2].start()
    row_hops[3].start()
    sides[1].start()
    col_keep().wait()
    over_cols(lambda t, z: col_in(t, z).wait_recv())
    for k in range(4):
        col_hops[k].start()
    arrange(0, 0)
    arrange(0, 1)
    for k, (land, d, half) in enumerate(arrivals):
        row_wait(land, d, half)
        if k < 2:
            row_hops[4 + k].start()
        sides[2 + k].start()
        col_wait(land, d, half)
        if k < 2:
            col_hops[4 + k].start()
        arrange(d, half)
    for k, (dy, half) in enumerate([(0, 0), (0, 1)] + [(dy, half) for _, dy, half in arrivals]):
        side(k, dy, half, 1).wait_recv()
    over_rows(lambda b, z: row_copy(b, z).wait_send())
    over_cols(lambda t, z: col_copy(t, z).wait_send())
    for copy in row_hops + col_hops + sides:
        copy.wait_send()


def panels_call(index, planes, factor):
    vmem = pl.BlockSpec(memory_space=pltpu.VMEM)
    dma = pltpu.SemaphoreType.DMA
    return pl.pallas_call(
        panels_kernel,
        name="panels",
        out_shape=(
            jax.ShapeDtypeStruct((8, RP, 256), BF),
            jax.ShapeDtypeStruct((2048, 2 * CP), BF),
        ),
        in_specs=[pl.BlockSpec(memory_space=pltpu.SMEM), vmem, vmem, vmem, vmem],
        out_specs=(vmem, vmem),
        scratch_shapes=[
            pltpu.VMEM((NBOX, 512), BF),
            pltpu.VMEM((NBOX, 512), F32),
            pltpu.VMEM((KB * NBOX, 128), F32),
            pltpu.VMEM((RP, 128), F32),
            pltpu.VMEM((NGRP, 16, RP), BF),
            pltpu.VMEM((NSLAB, 16, CP), BF),
            pltpu.VMEM((2, NGRP, 16, RP), BF),
            pltpu.VMEM((4, 2, NSLAB, 16, CP), BF),
            dma((NGRP, 2)),
            dma((2, NGRP)),
            dma((NSLAB, 2)),
            dma((2, NSLAB)),
            dma((6,)),
            dma((6,)),
            dma((6,)),
            dma((6,)),
            dma((8,)),
            dma((8,)),
            dma((2,)),
        ],
        compiler_params=pltpu.CompilerParams(
            collective_id=1, has_side_effects=True, vmem_limit_bytes=28 * 1024 * 1024
        ),
    )(index, planes, jnp.asarray(box_weights()), jnp.asarray(lane_order()), factor)


def tile_kernel(rp_ref, cab_ref, out_ref):
    rows = pl.ds(pl.multiple_of(pl.program_id(0) * 256, 256), 256)
    left = jnp.concatenate([rp_ref[k, rows, :] for k in range(8)], 1)
    o = jnp.dot(left, cab_ref[...], preferred_element_type=F32)
    out_ref[:, 0, :] = o[:, 0:CB]
    out_ref[:, 1, :] = o[:, CP : CP + CB]


def tile_call(row_panel, column_panel):
    rows = 256
    tiles = pl.pallas_call(
        tile_kernel,
        name="tile",
        grid=(RP // rows,),
        out_shape=jax.ShapeDtypeStruct((RB, 2, CB), F32),
        in_specs=[
            pl.BlockSpec((8, RP, 256), lambda i: (0, 0, 0)),
            pl.BlockSpec((2048, 2 * CP), lambda i: (0, 0)),
        ],
        out_specs=pl.BlockSpec((rows, 2, CB), lambda i: (i, 0, 0)),
        compiler_params=pltpu.CompilerParams(vmem_limit_bytes=32 * 1024 * 1024),
    )(row_panel, column_panel)
    return jnp.transpose(tiles, (1, 0, 2))


def table_look_up(index, table):
    hot = index[:, None] == jnp.arange(KB, dtype=jnp.int32)[None, :]
    return jnp.sum(jnp.where(hot, jnp.asarray(table)[None, :], 0), 1)


def on_device(
    valence_waves, conduction_waves, valence_energy, conduction_energy, occupation, gvec_ids
):
    g, gat = place_in_groups()
    s = lax.axis_index("slab")
    row, shifted = row_tables()
    along_x = gvec_ids // (KB * KB)
    along_y = gvec_ids // KB % KB
    along_z = gvec_ids % KB
    place = table_look_up(along_y, row * KB + shifted * 1024 * KB)
    index = (along_z ^ (place // (1024 * KB))) * NBOX + place % (1024 * KB) + along_x

    bands = [(0, 0), (0, 1), (-1, 0), (1, 0), (-1, 1), (1, 1), (2, 0), (2, 1)]
    order = jnp.stack([gat(*spot) for spot in bands])
    hot = (order[:, None] == jnp.arange(NV, dtype=jnp.int32)[None, :]).astype(F32)
    full = occupation.astype(F32)[:, None] / (
        (valence_energy[:, None] - conduction_energy[None, :]) * math.sqrt(NV * NC)
    )
    mine = jnp.sum(jnp.where(jnp.arange(NSLAB)[None, :] == s, full, 0.0), 1)
    factor = jnp.sum(hot * mine[None, :], 1)
    factor = jnp.broadcast_to(jnp.concatenate([factor, factor])[:, None], (16, 128))

    planes = planes_call(valence_waves, conduction_waves)
    row_panel, column_panel = panels_call(index, planes, factor)
    return tile_call(row_panel, column_panel)


def solution(mesh):
    in_specs = (P("grp", "slab", None, None), P("grp", "slab", None, None), P(), P("grp"), P(), P())
    out_specs = P(None, "grp", "slab")
    return jax.shard_map(
        on_device, mesh=mesh, in_specs=in_specs, out_specs=out_specs, check_vma=False
    )
```

profile of v0, /device:TPU:1, one launch (start us, length us, event | category | flops | bytes accessed | tf_op | source)
XLA Modules:
  0.0 158.1 jit_solution(12372390637750357210)
XLA Ops:
  0.0 0.1 stack.35
  0.1 0.7 convert_element_type.4
  0.8 0.9 select_reduce_fusion.2
  1.6 0.2 select_reduce_fusion.1
  1.8 0.1 pad_maximum_fusion
  1.9 0.1 broadcast_in_dim.44.fac_ref
  1.9 0.9 add_select_fusion.3
  2.8 1.0 select_reduce_fusion
  3.8 0.9 fusion.3.idx_ref
  4.7 0.0 copy-start.1
  4.7 0.0 copy-start.2
  4.7 75.6 %planes.1.in_ref = bf16[2,2,16,12,16,128]{5,4,3,2,1,0:T(8,128)(2,1)} custom-call(bf16[1,8,128,256]{3,2,1,0:T(8,128)(2,1)} %val_ref.1, bf16[16,8,128,256]{3,2,1,0:T(8,128)(2,1)} %con_ref.1, bf16[1024,256]{1,0:T(8,128)(2,1)} %constant.127.clone.wz_ref, bf16[64,128]{1,0:T(8,128)(2,1)} %constant.128.clone.ty_ref, f32[8,128]{1,0:T(8,128)} %constant.129.clone.mask_ref), custom_call_target="tpu_custom_call" | custom-call | tf_op jit(solution)/shard_map/planes/pallas_call | solution.py:340
  80.3 0.0 copy-done.1
  80.4 0.0 copy-done.2
  80.4 0.0 copy-start
  80.4 1.9 %copy-done = bf16[2,2,16,12,16,128]{5,4,3,2,1,0:T(8,128)(2,1)S(1)} copy-done((bf16[2,2,16,12,16,128]{5,4,3,2,1,0:T(8,128)(2,1)S(1)}, bf16[2,2,16,12,16,128]{5,4,3,2,1,0:T(8,128)(2,1)}, u32[]{:S(2)}) %copy-start) | copy-done | bytes 3145752
  82.3 63.2 %panels.1 = (bf16[8,1536,256]{2,1,0:T(8,128)(2,1)S(1)}, bf16[2048,1536]{1,0:T(8,128)(2,1)S(1)}) custom-call(s32[12000]{0:T(1024)S(1)} %fusion.3.idx_ref, bf16[2,2,16,12,16,128]{5,4,3,2,1,0:T(8,128)(2,1)S(1)} %copy-done, bf16[256,512]{1,0:T(8,128)(2,1)S(1)} %copy-done.2, bf16[512,512]{1,0:T(8,128)(2,1)S(1)} %copy-done.1, f32[16,128]{1,0:T(8,128)S(1)} %broadcast_in_dim.44.fac_ref), custom_call_target="tpu_custom_call" | custom-call | tf_op jit(solution)/shard_map/panels/pallas_call | solution.py:601
  145.4 12.6 %tile.1 = f32[1500,2,750]{2,1,0:T(2,128)} custom-call(bf16[8,1536,256]{2,1,0:T(8,128)(2,1)S(1)} %get-tuple-element.7.rp_ref, bf16[2048,1536]{1,0:T(8,128)(2,1)S(1)} %get-tuple-element.8.cab_ref), custom_call_target="tpu_custom_call" | custom-call | tf_op jit(solution)/shard_map/tile/pallas_call | solution.py:647
  (1 shorter events, 0.0 us)
Async XLA Ops:
  4.7 75.6 %copy-start.1 = (bf16[512,512]{1,0:T(8,128)(2,1)S(1)}, bf16[512,512]{1,0:T(8,128)(2,1)}, u32[]{:S(2)}) copy-start(bf16[512,512]{1,0:T(8,128)(2,1)} %constant.131.clone.order_ref) | copy-start | bytes 1572868
  4.7 75.6 %copy-start.2 = (bf16[256,512]{1,0:T(8,128)(2,1)S(1)}, bf16[256,512]{1,0:T(8,128)(2,1)}, u32[]{:S(2)}) copy-start(bf16[256,512]{1,0:T(8,128)(2,1)} %constant.130.clone.tab_ref) | copy-start | bytes 786436
  80.4 1.9 %copy-start = (bf16[2,2,16,12,16,128]{5,4,3,2,1,0:T(8,128)(2,1)S(1)}, bf16[2,2,16,12,16,128]{5,4,3,2,1,0:T(8,128)(2,1)}, u32[]{:S(2)}) copy-start(bf16[2,2,16,12,16,128]{5,4,3,2,1,0:T(8,128)(2,1)} %planes.1.in_ref) | copy-start | bytes 9437188
where the time goes:
time: 158 us
  Pallas kernels  151 us (96%)
  other arithmetic  4.54 us (3%)
  local copies, waits for them, and re-layouts  2.05 us (1%)
    pallas_call x1, Pallas kernels, planes_call(): pl.pallas_call(planes_kernel, name='planes', out_shape=jax.ShapeDtypeStru...  75.6 us
    pallas_call x1, Pallas kernels, panels_call(): pl.pallas_call(panels_kernel, name='panels', out_shape=(jax.ShapeDtypeStr...  63.2 us
    pallas_call x1, Pallas kernels, tile_call(): pl.pallas_call(tile_kernel, name='tile', grid=(RP // rows,), out_shape=ja...  12.6 us

commit v1 on v0

--- a/solution.py
+++ b/solution.py
@@ -375,14 +375,14 @@
 
 
 def panels_kernel(
-    idx_ref, in_ref, tab_ref, order_ref, fac_ref, rp_ref, cab_ref,
-    xb, wide, box, blk, rows, cols, landed, cp,
+    idx_ref, ve_ref, ce_ref, oc_ref, in_ref, tab_ref, order_ref, acc_ref, left_ref, right_ref,
+    rp_ref, cab_ref, xb, wide, box, blk, rows, cols, landed, cp,
     rsa, rra, csa, cra, rs, rr, cs, cr, sib_s, sib_r, lsem,
 ):
     g, gat = place_in_groups()
     s, sat = place_in_slabs()
     gx, gz = g // 2, lax.rem(g, 2)
-    sz, yc = s // 8, lax.rem(s, 8)
+    sz, yc, sc = s // 8, lax.rem(s, 8), lax.rem(s, 2)
     scaling = 0.5 / float(NF) ** 1.5
 
     barrier = pltpu.get_barrier_semaphore()
@@ -421,6 +421,15 @@
 
     lax.fori_loop(0, NBOX // 96, spread, 0)
     blk[1496:1536, :] = jnp.zeros((40, 128), F32)
+    for chunk in range(6):
+        cab_ref[chunk * 256 + 128 : chunk * 256 + 192, :] = jnp.zeros((64, 2 * CP), BF)
+    slot = lax.rem(lax.broadcasted_iota(jnp.int32, (16, CP), 0), 8)
+    charge, gap = jnp.zeros((16, CP), F32), jnp.ones((16, CP), F32)
+    for place, spot in enumerate([(0, 0), (0, 1), (-1, 0), (1, 0), (-1, 1), (1, 1), (2, 0), (2, 1)]):
+        v = gat(*spot)
+        charge = jnp.where(slot == place, oc_ref[v].astype(F32), charge)
+        gap = jnp.where(slot == place, ve_ref[v] - ce_ref[s], gap)
+    factor = (charge / (gap * math.sqrt(NV * NC)))[:, 0:1]
     pl.semaphore_wait(barrier, 43)
 
     lane = lax.broadcasted_iota(jnp.int32, (16, 128), 1)
@@ -430,14 +439,16 @@
 
     def row_copy(b, z):
         to = {"grp": b, "slab": z * 8 + yc}
-        return remote(rows.at[b], landed.at[sz, g], rsa.at[b, z], rra.at[sz, g], to)
+        dx = lax.rem(gx - b // 2 + 4, 4)
+        return remote(rows.at[b], landed.at[dx, gz, sz], rsa.at[b, z], rra.at[dx, gz, sz], to)
 
     def row_in(b, z):
         to = {"grp": b, "slab": z * 8 + yc}
-        return remote(rows.at[b], landed.at[z, b], rsa.at[b, z], rra.at[z, b], to)
+        dx, bz = lax.rem(b // 2 - gx + 4, 4), lax.rem(b, 2)
+        return remote(rows.at[b], landed.at[dx, bz, z], rsa.at[b, z], rra.at[dx, bz, z], to)
 
     def row_keep():
-        return pltpu.make_async_copy(rows.at[g], landed.at[sz, g], lsem.at[0])
+        return pltpu.make_async_copy(rows.at[g], landed.at[0, gz, sz], lsem.at[0])
 
     def col_copy(t, z):
         to = {"grp": gx * 2 + z, "slab": t}
@@ -461,7 +472,7 @@
 
         lax.fori_loop(0, RB // 60, pick, 0)
         o = lax.dot_general(unit, blk[0:RP, :].astype(BF), contract, preferred_element_type=F32)
-        rows[b] = (o * fac_ref[:, 0:1]).astype(BF)
+        rows[b] = (o * factor).astype(BF)
         for half in range(2):
             part = blk[half * CB : half * CB + CP, :].astype(BF)
             cols[2 * b + half] = lax.dot_general(unit, part, contract, preferred_element_type=F32).astype(BF)
@@ -516,11 +527,13 @@
         lax.fori_loop(0, 2 * NSLAB, step, 0)
 
     def row_part(dy, dc, half):
-        return rp_ref.at[sat(dy, 0, dc) % 8, pl.ds(half * 768, 768)]
+        return rp_ref.at[PLACE[dy], lax.rem(sc + dc, 2), pl.ds(half * 768, 768)]
 
     def row_hop(k, dy, half, to, land):
-        part = row_part(dy, 0, half)
-        return remote(part, part, rs.at[k], rr.at[land], {"slab": sat(to, 0, 0)})
+        there = dy - to if dy - to > -2 else 2
+        return remote(
+            row_part(dy, 0, half), row_part(there, 0, half), rs.at[k], rr.at[land], {"slab": sat(to, 0, 0)}
+        )
 
     def row_wait(land, dy, half):
         part = row_part(dy, 0, half)
@@ -543,28 +556,36 @@
 
     hops = [(0, 0, 1, 0), (0, 1, -1, 3), (0, 1, 1, 1), (0, 0, -1, 2), (-1, 0, 1, 4), (1, 1, -1, 5)]
     arrivals = [(0, -1, 0), (3, 1, 1), (1, -1, 1), (2, 1, 0), (4, 2, 0), (5, 2, 1)]
+    own_and_near = [(0, 0), (0, 1)] + [(dy, half) for _, dy, half in arrivals]
     row_hops = [row_hop(k, *hop) for k, hop in enumerate(hops)]
     col_hops = [col_hop(k, *hop) for k, hop in enumerate(hops)]
     sides = [side(0, 0, 0), side(1, 0, 1)] + [side(2 + k, dy, half) for k, (_, dy, half) in enumerate(arrivals)]
 
     def arrange(dx, half):
         x = gat(dx, 0) // 2
-
-        def step(t, _):
-            part = cp[x, half, pl.ds(t, 1)].reshape(16, CP)
-            put = pl.multiple_of(lax.rem(t, 8) * 256 + (t // 8) * 128 + x * 32 + half * 16, 16)
-            cab_ref[pl.ds(put, 16), 0:CP] = part
-            value = part.astype(F32)
-            cab_ref[pl.ds(put, 16), CP : 2 * CP] = jnp.concatenate([-value[8:16], value[0:8]], 0).astype(BF)
-            return 0
-
-        lax.fori_loop(0, NSLAB, step, 0)
+        for dy in (0, -1, 1, 2):
+            for dc in range(2):
+                chunk = PLACE[dy] * 2 + dc
+                for z in range(2):
+                    t = z * 8 + lax.rem(yc // 2 + dy + 4, 4) * 2 + dc
+                    part = cp[x, half, pl.ds(t, 1)].reshape(16, CP)
+                    value = part.astype(F32)
+                    turned = jnp.concatenate([-value[8:16], value[0:8]], 0).astype(BF)
+                    put = (dx % 4) * 64 + half * 32 + z * 16
+                    if dy == 2:
+                        to, put = right_ref, dc * 256 + put
+                    elif dx == 2:
+                        to, put = right_ref, 512 + chunk * 64 + half * 32 + z * 16
+                    else:
+                        to, put = cab_ref, chunk * 256 + put
+                    to[put : put + 16, 0:CP] = part
+                    to[put : put + 16, CP : 2 * CP] = turned
 
     row_keep().wait()
     over_rows(lambda b, z: row_in(b, z).wait_recv())
     for j in range(RP // 128):
-        part = landed[:, :, :, j * 128 : (j + 1) * 128].reshape(256, 128).astype(F32)
-        rp_ref[yc, j * 128 : (j + 1) * 128, :] = part.T.astype(BF)
+        part = landed[:, :, :, :, j * 128 : (j + 1) * 128].reshape(256, 128).astype(F32)
+        rp_ref[0, sc, j * 128 : (j + 1) * 128, :] = part.T.astype(BF)
         if j == 5:
             row_hops[0].start()
             sides[0].start()
@@ -587,37 +608,60 @@
         if k < 2:
             col_hops[4 + k].start()
         arrange(d, half)
-    for k, (dy, half) in enumerate([(0, 0), (0, 1)] + [(dy, half) for _, dy, half in arrivals]):
-        side(k, dy, half, 1).wait_recv()
+        if k == 3:
+            for n in range(6):
+                side(n, *own_and_near[n], 1).wait_recv()
+
+            def near(m, _):
+                put = pl.ds(pl.multiple_of(m * 256, 256), 256)
+                parts = [rp_ref[p, c, put, :] for p in range(3) for c in range(2)]
+                acc_ref[put, :] = jnp.dot(jnp.concatenate(parts, 1), cab_ref[...], preferred_element_type=F32)
+                for pair in range(3):
+                    both = [parts[2 * pair][:, 128:192], parts[2 * pair + 1][:, 128:192]]
+                    left_ref[put, 512 + pair * 128 : 640 + pair * 128] = jnp.concatenate(both, 1)
+                return 0
+
+            lax.fori_loop(0, RP // 256, near, 0)
+    for n in range(6, 8):
+        side(n, *own_and_near[n], 1).wait_recv()
+    for c in range(2):
+        left_ref[:, c * 256 : c * 256 + 256] = rp_ref[3, c]
     over_rows(lambda b, z: row_copy(b, z).wait_send())
     over_cols(lambda t, z: col_copy(t, z).wait_send())
     for copy in row_hops + col_hops + sides:
         copy.wait_send()
 
 
-def panels_call(index, planes, factor):
+PLACE = {0: 0, -1: 1, 1: 2, 2: 3}
+
+
+def panels_call(index, planes, valence_energy, conduction_energy, occupation):
+    smem = pl.BlockSpec(memory_space=pltpu.SMEM)
     vmem = pl.BlockSpec(memory_space=pltpu.VMEM)
     dma = pltpu.SemaphoreType.DMA
     return pl.pallas_call(
         panels_kernel,
         name="panels",
         out_shape=(
-            jax.ShapeDtypeStruct((8, RP, 256), BF),
-            jax.ShapeDtypeStruct((2048, 2 * CP), BF),
+            jax.ShapeDtypeStruct((RP, 2 * CP), F32),
+            jax.ShapeDtypeStruct((RP, 896), BF),
+            jax.ShapeDtypeStruct((896, 2 * CP), BF),
         ),
-        in_specs=[pl.BlockSpec(memory_space=pltpu.SMEM), vmem, vmem, vmem, vmem],
-        out_specs=(vmem, vmem),
+        in_specs=[smem, smem, smem, smem, vmem, vmem, vmem],
+        out_specs=(vmem, vmem, vmem),
         scratch_shapes=[
+            pltpu.VMEM((4, 2, RP, 256), BF),
+            pltpu.VMEM((1536, 2 * CP), BF),
             pltpu.VMEM((NBOX, 512), BF),
             pltpu.VMEM((NBOX, 512), F32),
             pltpu.VMEM((KB * NBOX, 128), F32),
             pltpu.VMEM((RP, 128), F32),
             pltpu.VMEM((NGRP, 16, RP), BF),
             pltpu.VMEM((NSLAB, 16, CP), BF),
-            pltpu.VMEM((2, NGRP, 16, RP), BF),
+            pltpu.VMEM((4, 2, 2, 16, RP), BF),
             pltpu.VMEM((4, 2, NSLAB, 16, CP), BF),
             dma((NGRP, 2)),
-            dma((2, NGRP)),
+            dma((4, 2, 2)),
             dma((NSLAB, 2)),
             dma((2, NSLAB)),
             dma((6,)),
@@ -629,20 +673,27 @@
             dma((2,)),
         ],
         compiler_params=pltpu.CompilerParams(
-            collective_id=1, has_side_effects=True, vmem_limit_bytes=28 * 1024 * 1024
+            collective_id=1, has_side_effects=True, vmem_limit_bytes=34 * 1024 * 1024
         ),
-    )(index, planes, jnp.asarray(box_weights()), jnp.asarray(lane_order()), factor)
-
-
-def tile_kernel(rp_ref, cab_ref, out_ref):
+    )(
+        index,
+        valence_energy,
+        conduction_energy,
+        occupation,
+        planes,
+        jnp.asarray(box_weights()),
+        jnp.asarray(lane_order()),
+    )
+
+
+def tile_kernel(acc_ref, left_ref, right_ref, out_ref):
     rows = pl.ds(pl.multiple_of(pl.program_id(0) * 256, 256), 256)
-    left = jnp.concatenate([rp_ref[k, rows, :] for k in range(8)], 1)
-    o = jnp.dot(left, cab_ref[...], preferred_element_type=F32)
+    o = jnp.dot(left_ref[rows, :], right_ref[...], preferred_element_type=F32) + acc_ref[rows, :]
     out_ref[:, 0, :] = o[:, 0:CB]
     out_ref[:, 1, :] = o[:, CP : CP + CB]
 
 
-def tile_call(row_panel, column_panel):
+def tile_call(near, left, right):
     rows = 256
     tiles = pl.pallas_call(
         tile_kernel,
@@ -650,25 +701,26 @@
         grid=(RP // rows,),
         out_shape=jax.ShapeDtypeStruct((RB, 2, CB), F32),
         in_specs=[
-            pl.BlockSpec((8, RP, 256), lambda i: (0, 0, 0)),
-            pl.BlockSpec((2048, 2 * CP), lambda i: (0, 0)),
+            pl.BlockSpec((RP, 2 * CP), lambda i: (0, 0)),
+            pl.BlockSpec((RP, 896), lambda i: (0, 0)),
+            pl.BlockSpec((896, 2 * CP), lambda i: (0, 0)),
         ],
         out_specs=pl.BlockSpec((rows, 2, CB), lambda i: (i, 0, 0)),
         compiler_params=pltpu.CompilerParams(vmem_limit_bytes=32 * 1024 * 1024),
-    )(row_panel, column_panel)
+    )(near, left, right)
     return jnp.transpose(tiles, (1, 0, 2))
 
 
 def table_look_up(index, table):
-    hot = index[:, None] == jnp.arange(KB, dtype=jnp.int32)[None, :]
-    return jnp.sum(jnp.where(hot, jnp.asarray(table)[None, :], 0), 1)
+    found = jnp.zeros_like(index)
+    for place, value in enumerate(table):
+        found = jnp.where(index == place, int(value), found)
+    return found
 
 
 def on_device(
     valence_waves, conduction_waves, valence_energy, conduction_energy, occupation, gvec_ids
 ):
-    g, gat = place_in_groups()
-    s = lax.axis_index("slab")
     row, shifted = row_tables()
     along_x = gvec_ids // (KB * KB)
     along_y = gvec_ids // KB % KB
@@ -676,19 +728,9 @@
     place = table_look_up(along_y, row * KB + shifted * 1024 * KB)
     index = (along_z ^ (place // (1024 * KB))) * NBOX + place % (1024 * KB) + along_x
 
-    bands = [(0, 0), (0, 1), (-1, 0), (1, 0), (-1, 1), (1, 1), (2, 0), (2, 1)]
-    order = jnp.stack([gat(*spot) for spot in bands])
-    hot = (order[:, None] == jnp.arange(NV, dtype=jnp.int32)[None, :]).astype(F32)
-    full = occupation.astype(F32)[:, None] / (
-        (valence_energy[:, None] - conduction_energy[None, :]) * math.sqrt(NV * NC)
-    )
-    mine = jnp.sum(jnp.where(jnp.arange(NSLAB)[None, :] == s, full, 0.0), 1)
-    factor = jnp.sum(hot * mine[None, :], 1)
-    factor = jnp.broadcast_to(jnp.concatenate([factor, factor])[:, None], (16, 128))
-
     planes = planes_call(valence_waves, conduction_waves)
-    row_panel, column_panel = panels_call(index, planes, factor)
-    return tile_call(row_panel, column_panel)
+    near, left, right = panels_call(index, planes, valence_energy, conduction_energy, occupation)
+    return tile_call(near, left, right)
 
 
 def solution(mesh):

time: 158 us -> 152 us (0.962)
  other arithmetic: 4.54 us -> 1.09 us
  Pallas kernels: 151 us -> 149 us
    pallas_call x1, Pallas kernels: 12.6 us -> 8.26 us  [tile_call(): pl.pallas_call(tile_kernel, name='tile', grid=(RP // rows,), out_shape=ja...]
    reduce_sum x3 -> x0, other arithmetic: 2.04 us -> none  [the longest x1 1 us: table_look_up(): return jnp.sum(jnp.where(hot, jnp.asarray(table)[None, :], 0), 1)]
    pallas_call x1, Pallas kernels: 63.2 us -> 65.2 us  [panels_call(): pl.pallas_call(panels_kernel, name='panels', out_shape=(jax.ShapeDtypeStr...]
where the time goes in v1:
time: 152 us
  Pallas kernels  149 us (98%)
  local copies, waits for them, and re-layouts  1.9 us (1%)
    pallas_call x1, Pallas kernels, planes_call(): pl.pallas_call(planes_kernel, name='planes', out_shape=jax.ShapeDtypeStru...  75.6 us
    pallas_call x1, Pallas kernels, panels_call(): pl.pallas_call(panels_kernel, name='panels', out_shape=(jax.ShapeDtypeStr...  65.2 us
    pallas_call x1, Pallas kernels, tile_call(): pl.pallas_call(tile_kernel, name='tile', grid=(RP // rows,), out_shape=ja...  8.26 us

profile of v1, /device:TPU:1, one launch (start us, length us, event | category | flops | bytes accessed | tf_op | source)
XLA Modules:
  0.0 152.2 jit_solution(15670104478452541248)
XLA Ops:
  0.0 0.0 copy-start.1
  0.0 0.0 copy-start.2
  0.0 0.0 copy-start.5
  0.0 0.0 copy-start.4
  0.0 0.0 copy-start.3
  0.0 1.1 fusion.3.idx_ref
  1.1 75.6 %planes.1.in_ref = bf16[2,2,16,12,16,128]{5,4,3,2,1,0:T(8,128)(2,1)} custom-call(bf16[1,8,128,256]{3,2,1,0:T(8,128)(2,1)} %val_ref.1, bf16[16,8,128,256]{3,2,1,0:T(8,128)(2,1)} %con_ref.1, bf16[1024,256]{1,0:T(8,128)(2,1)} %constant.192.clone.wz_ref, bf16[64,128]{1,0:T(8,128)(2,1)} %constant.193.clone.ty_ref, f32[8,128]{1,0:T(8,128)} %constant.194.clone.mask_ref), custom_call_target="tpu_custom_call" | custom-call | tf_op jit(solution)/shard_map/planes/pallas_call | solution.py:340
  76.8 0.0 copy-done.1
  76.8 0.0 copy-done.2
  76.8 0.0 copy-done.5
  76.8 0.0 copy-done.4
  76.8 0.0 copy-done.3
  76.8 0.0 copy-start
  76.8 1.9 %copy-done = bf16[2,2,16,12,16,128]{5,4,3,2,1,0:T(8,128)(2,1)S(1)} copy-done((bf16[2,2,16,12,16,128]{5,4,3,2,1,0:T(8,128)(2,1)S(1)}, bf16[2,2,16,12,16,128]{5,4,3,2,1,0:T(8,128)(2,1)}, u32[]{:S(2)}) %copy-start) | copy-done | bytes 3145752
  78.7 65.2 %panels.1 = (f32[1536,1536]{1,0:T(8,128)S(1)}, bf16[1536,896]{1,0:T(8,128)(2,1)S(1)}, bf16[896,1536]{1,0:T(8,128)(2,1)S(1)}) custom-call(s32[12000]{0:T(1024)S(1)} %fusion.3.idx_ref, f32[8]{0:T(128)S(1)} %copy-done.3, f32[16]{0:T(128)S(1)} %copy-done.4, s32[8]{0:T(128)S(1)} %copy-done.5, bf16[2,2,16,12,16,128]{5,4,3,2,1,0:T(8,128)(2,1)S(1)} %copy-done, ...), custom_call_target="tpu_custom_call" | custom-call | tf_op jit(solution)/shard_map/panels/pallas_call | solution.py:642
  143.9 8.3 %tile.1 = f32[1500,2,750]{2,1,0:T(2,128)} custom-call(f32[1536,1536]{1,0:T(8,128)S(1)} %get-tuple-element.8.acc_ref, bf16[1536,896]{1,0:T(8,128)(2,1)S(1)} %get-tuple-element.9.left_ref, bf16[896,1536]{1,0:T(8,128)(2,1)S(1)} %get-tuple-element.10.right_ref), custom_call_target="tpu_custom_call" | custom-call | tf_op jit(solution)/shard_map/tile/pallas_call | solution.py:698
Async XLA Ops:
  0.0 76.8 %copy-start.1 = (bf16[512,512]{1,0:T(8,128)(2,1)S(1)}, bf16[512,512]{1,0:T(8,128)(2,1)}, u32[]{:S(2)}) copy-start(bf16[512,512]{1,0:T(8,128)(2,1)} %constant.196.clone.order_ref) | copy-start | bytes 1572868
  0.0 76.8 %copy-start.2 = (bf16[256,512]{1,0:T(8,128)(2,1)S(1)}, bf16[256,512]{1,0:T(8,128)(2,1)}, u32[]{:S(2)}) copy-start(bf16[256,512]{1,0:T(8,128)(2,1)} %constant.195.clone.tab_ref) | copy-start | bytes 786436
  0.0 76.8 %copy-start.5 = (s32[8]{0:T(128)S(1)}, s32[8]{0:T(128)}, u32[]{:S(2)}) copy-start(s32[8]{0:T(128)} %oc_ref.1) | copy-start | bytes 100
  0.0 76.8 %copy-start.4 = (f32[16]{0:T(128)S(1)}, f32[16]{0:T(128)}, u32[]{:S(2)}) copy-start(f32[16]{0:T(128)} %ce_ref.1) | copy-start | bytes 196
  0.0 76.8 %copy-start.3 = (f32[8]{0:T(128)S(1)}, f32[8]{0:T(128)}, u32[]{:S(2)}) copy-start(f32[8]{0:T(128)} %ve_ref.1) | copy-start | bytes 100
  76.8 1.9 %copy-start = (bf16[2,2,16,12,16,128]{5,4,3,2,1,0:T(8,128)(2,1)S(1)}, bf16[2,2,16,12,16,128]{5,4,3,2,1,0:T(8,128)(2,1)}, u32[]{:S(2)}) copy-start(bf16[2,2,16,12,16,128]{5,4,3,2,1,0:T(8,128)(2,1)} %planes.1.in_ref) | copy-start | bytes 9437188

commit v2 on v1

--- a/solution.py
+++ b/solution.py
@@ -420,7 +420,7 @@
         return 0
 
     lax.fori_loop(0, NBOX // 96, spread, 0)
-    blk[1496:1536, :] = jnp.zeros((40, 128), F32)
+    blk[CP : CP + 32, :] = jnp.zeros((32, 128), F32)
     for chunk in range(6):
         cab_ref[chunk * 256 + 128 : chunk * 256 + 192, :] = jnp.zeros((64, 2 * CP), BF)
     slot = lax.rem(lax.broadcasted_iota(jnp.int32, (16, CP), 0), 8)
@@ -437,18 +437,18 @@
     unit = jnp.where(lane == row, 1.0, 0.0).astype(BF)
     contract = (((1,), (1,)), ((), ()))
 
-    def row_copy(b, z):
+    def row_copy(h, b, z):
         to = {"grp": b, "slab": z * 8 + yc}
         dx = lax.rem(gx - b // 2 + 4, 4)
-        return remote(rows.at[b], landed.at[dx, gz, sz], rsa.at[b, z], rra.at[dx, gz, sz], to)
-
-    def row_in(b, z):
+        return remote(rows.at[h, b], landed.at[h, dx, gz, sz], rsa.at[h, b, z], rra.at[h, dx, gz, sz], to)
+
+    def row_in(h, b, z):
         to = {"grp": b, "slab": z * 8 + yc}
         dx, bz = lax.rem(b // 2 - gx + 4, 4), lax.rem(b, 2)
-        return remote(rows.at[b], landed.at[dx, bz, z], rsa.at[b, z], rra.at[dx, bz, z], to)
-
-    def row_keep():
-        return pltpu.make_async_copy(rows.at[g], landed.at[0, gz, sz], lsem.at[0])
+        return remote(rows.at[h, b], landed.at[h, dx, bz, z], rsa.at[h, b, z], rra.at[h, dx, bz, z], to)
+
+    def row_keep(h):
+        return pltpu.make_async_copy(rows.at[h, g], landed.at[h, 0, gz, sz], lsem.at[h])
 
     def col_copy(t, z):
         to = {"grp": gx * 2 + z, "slab": t}
@@ -459,48 +459,53 @@
         return remote(cols.at[t], cp.at[gx, z, t], csa.at[t, z], cra.at[z, t], to)
 
     def col_keep():
-        return pltpu.make_async_copy(cols.at[s], cp.at[gx, gz, s], lsem.at[1])
-
-    def one_block(i, _):
+        return pltpu.make_async_copy(cols.at[s], cp.at[gx, gz, s], lsem.at[2])
+
+    def one_block(h, i):
         b = lax.rem(g + yc // 2 + sz * 4 + i, NGRP)
+        count, many = (CP, 64) if h == 0 else (CB, 50)
+        origin = b * RB + h * CB
 
         def pick(j, _):
-            base = j * 60
-            for k in range(60):
-                blk[pl.ds(base + k, 1), :] = box[pl.ds(idx_ref[b * RB + base + k], 1), :]
+            base = j * many
+            for k in range(many):
+                blk[pl.ds(base + k, 1), :] = box[pl.ds(idx_ref[origin + base + k], 1), :]
             return 0
 
-        lax.fori_loop(0, RB // 60, pick, 0)
-        o = lax.dot_general(unit, blk[0:RP, :].astype(BF), contract, preferred_element_type=F32)
-        rows[b] = (o * factor).astype(BF)
-        for half in range(2):
-            part = blk[half * CB : half * CB + CP, :].astype(BF)
-            cols[2 * b + half] = lax.dot_general(unit, part, contract, preferred_element_type=F32).astype(BF)
+        lax.fori_loop(0, count // many, pick, 0)
+        skip = h * (CP - CB)
+        o = lax.dot_general(unit, blk[skip : skip + CP, :].astype(BF), contract, preferred_element_type=F32)
+        rows[h, b] = (o * factor).astype(BF)
+        o = lax.dot_general(unit, blk[0:CP, :].astype(BF), contract, preferred_element_type=F32)
+        cols[2 * b + h] = o.astype(BF)
         for z in range(2):
             mine = jnp.logical_and(b == g, z == sz)
 
             @pl.when(mine)
             def _():
-                row_keep().start()
+                row_keep(h).start()
 
             @pl.when(jnp.logical_not(mine))
             def _():
-                row_copy(b, z).start()
-
-            for half in range(2):
-                own = jnp.logical_and(2 * b + half == s, z == gz)
-
-                @pl.when(own)
-                def _():
-                    col_keep().start()
-
-                @pl.when(jnp.logical_not(own))
-                def _():
-                    col_copy(2 * b + half, z).start()
-
-        return 0
-
-    lax.fori_loop(0, NGRP, one_block, 0)
+                row_copy(h, b, z).start()
+
+            own = jnp.logical_and(2 * b + h == s, z == gz)
+
+            @pl.when(own)
+            def _():
+                col_keep().start()
+
+            @pl.when(jnp.logical_not(own))
+            def _():
+                col_copy(2 * b + h, z).start()
+
+    for h in range(2):
+
+        def block_step(i, _):
+            one_block(h, i)
+            return 0
+
+        lax.fori_loop(0, NGRP, block_step, 0)
 
     def over_rows(act):
         def step(i, _):
@@ -555,7 +560,7 @@
         remote(part, part, cs.at[0], cr.at[land], {"grp": gat(1, 0)}).wait_recv()
 
     hops = [(0, 0, 1, 0), (0, 1, -1, 3), (0, 1, 1, 1), (0, 0, -1, 2), (-1, 0, 1, 4), (1, 1, -1, 5)]
-    arrivals = [(0, -1, 0), (3, 1, 1), (1, -1, 1), (2, 1, 0), (4, 2, 0), (5, 2, 1)]
+    arrivals = [(0, -1, 0), (2, 1, 0), (3, 1, 1), (1, -1, 1), (4, 2, 0), (5, 2, 1)]
     own_and_near = [(0, 0), (0, 1)] + [(dy, half) for _, dy, half in arrivals]
     row_hops = [row_hop(k, *hop) for k, hop in enumerate(hops)]
     col_hops = [col_hop(k, *hop) for k, hop in enumerate(hops)]
@@ -581,32 +586,36 @@
                     to[put : put + 16, 0:CP] = part
                     to[put : put + 16, CP : 2 * CP] = turned
 
-    row_keep().wait()
-    over_rows(lambda b, z: row_in(b, z).wait_recv())
-    for j in range(RP // 128):
-        part = landed[:, :, :, :, j * 128 : (j + 1) * 128].reshape(256, 128).astype(F32)
-        rp_ref[0, sc, j * 128 : (j + 1) * 128, :] = part.T.astype(BF)
-        if j == 5:
-            row_hops[0].start()
-            sides[0].start()
-    row_hops[1].start()
-    row_hops[2].start()
-    row_hops[3].start()
-    sides[1].start()
-    col_keep().wait()
-    over_cols(lambda t, z: col_in(t, z).wait_recv())
-    for k in range(4):
-        col_hops[k].start()
+    def own_columns():
+        col_keep().wait()
+        over_cols(lambda t, z: col_in(t, z).wait_recv())
+        for k in (0, 3, 1, 2):
+            col_hops[k].start()
+
+    for h in range(2):
+        row_keep(h).wait()
+        over_rows(lambda b, z: row_in(h, b, z).wait_recv())
+        for j in range(CP // 128):
+            part = landed[h, :, :, :, :, j * 128 : (j + 1) * 128].reshape(256, 128).astype(F32)
+            rp_ref[0, sc, h * CP + j * 128 : h * CP + (j + 1) * 128, :] = part.T.astype(BF)
+        for k in ((0, 3), (1, 2))[h]:
+            row_hops[k].start()
+        sides[h].start()
+
+        @pl.when(sc == h)
+        def _():
+            own_columns()
+
     arrange(0, 0)
     arrange(0, 1)
     for k, (land, d, half) in enumerate(arrivals):
         row_wait(land, d, half)
-        if k < 2:
-            row_hops[4 + k].start()
+        if k in (0, 2):
+            row_hops[4 + k // 2].start()
         sides[2 + k].start()
         col_wait(land, d, half)
-        if k < 2:
-            col_hops[4 + k].start()
+        if k in (0, 2):
+            col_hops[4 + k // 2].start()
         arrange(d, half)
         if k == 3:
             for n in range(6):
@@ -626,7 +635,8 @@
         side(n, *own_and_near[n], 1).wait_recv()
     for c in range(2):
         left_ref[:, c * 256 : c * 256 + 256] = rp_ref[3, c]
-    over_rows(lambda b, z: row_copy(b, z).wait_send())
+    for h in range(2):
+        over_rows(lambda b, z: row_copy(h, b, z).wait_send())
     over_cols(lambda t, z: col_copy(t, z).wait_send())
     for copy in row_hops + col_hops + sides:
         copy.wait_send()
@@ -655,13 +665,13 @@
             pltpu.VMEM((NBOX, 512), BF),
             pltpu.VMEM((NBOX, 512), F32),
             pltpu.VMEM((KB * NBOX, 128), F32),
-            pltpu.VMEM((RP, 128), F32),
-            pltpu.VMEM((NGRP, 16, RP), BF),
+            pltpu.VMEM((CP + 32, 128), F32),
+            pltpu.VMEM((2, NGRP, 16, CP), BF),
             pltpu.VMEM((NSLAB, 16, CP), BF),
-            pltpu.VMEM((4, 2, 2, 16, RP), BF),
+            pltpu.VMEM((2, 4, 2, 2, 16, CP), BF),
             pltpu.VMEM((4, 2, NSLAB, 16, CP), BF),
-            dma((NGRP, 2)),
-            dma((4, 2, 2)),
+            dma((2, NGRP, 2)),
+            dma((2, 4, 2, 2)),
             dma((NSLAB, 2)),
             dma((2, NSLAB)),
             dma((6,)),
@@ -670,7 +680,7 @@
             dma((6,)),
             dma((8,)),
             dma((8,)),
-            dma((2,)),
+            dma((3,)),
         ],
         compiler_params=pltpu.CompilerParams(
             collective_id=1, has_side_effects=True, vmem_limit_bytes=34 * 1024 * 1024

time: 152 us -> 150 us (0.987)
  Pallas kernels: 149 us -> 146 us
    pallas_call x1, Pallas kernels: 65.2 us -> 62.1 us  [panels_call(): pl.pallas_call(panels_kernel, name='panels', out_shape=(jax.ShapeDtypeStr...]
where the time goes in v2:
time: 150 us; the launch traced here: 149 us
  Pallas kernels  146 us (97%)
  local copies, waits for them, and re-layouts  1.9 us (1%)
    pallas_call x1, Pallas kernels, planes_call(): pl.pallas_call(planes_kernel, name='planes', out_shape=jax.ShapeDtypeStru...  75.6 us
    pallas_call x1, Pallas kernels, panels_call(): pl.pallas_call(panels_kernel, name='panels', out_shape=(jax.ShapeDtypeStr...  62.1 us
    pallas_call x1, Pallas kernels, tile_call(): pl.pallas_call(tile_kernel, name='tile', grid=(RP // rows,), out_shape=ja...  8.25 us

profile of v2, /device:TPU:1, one launch (start us, length us, event | category | flops | bytes accessed | tf_op | source)
XLA Modules:
  0.0 149.0 jit_solution(14746496139902610931)
XLA Ops:
  0.0 0.0 copy-start.1
  0.0 0.0 copy-start.2
  0.0 0.0 copy-start.5
  0.0 0.0 copy-start.4
  0.0 0.0 copy-start.3
  0.0 1.1 fusion.3.idx_ref
  1.1 75.6 %planes.1.in_ref = bf16[2,2,16,12,16,128]{5,4,3,2,1,0:T(8,128)(2,1)} custom-call(bf16[1,8,128,256]{3,2,1,0:T(8,128)(2,1)} %val_ref.1, bf16[16,8,128,256]{3,2,1,0:T(8,128)(2,1)} %con_ref.1, bf16[1024,256]{1,0:T(8,128)(2,1)} %constant.192.clone.wz_ref, bf16[64,128]{1,0:T(8,128)(2,1)} %constant.193.clone.ty_ref, f32[8,128]{1,0:T(8,128)} %constant.194.clone.mask_ref), custom_call_target="tpu_custom_call" | custom-call | tf_op jit(solution)/shard_map/planes/pallas_call | solution.py:340
  76.7 0.0 copy-done.1
  76.7 0.0 copy-done.2
  76.7 0.0 copy-done.5
  76.7 0.0 copy-done.4
  76.7 0.0 copy-done.3
  76.7 0.0 copy-start
  76.7 1.9 %copy-done = bf16[2,2,16,12,16,128]{5,4,3,2,1,0:T(8,128)(2,1)S(1)} copy-done((bf16[2,2,16,12,16,128]{5,4,3,2,1,0:T(8,128)(2,1)S(1)}, bf16[2,2,16,12,16,128]{5,4,3,2,1,0:T(8,128)(2,1)}, u32[]{:S(2)}) %copy-start) | copy-done | bytes 3145752
  78.6 62.1 %panels.1 = (f32[1536,1536]{1,0:T(8,128)S(1)}, bf16[1536,896]{1,0:T(8,128)(2,1)S(1)}, bf16[896,1536]{1,0:T(8,128)(2,1)S(1)}) custom-call(s32[12000]{0:T(1024)S(1)} %fusion.3.idx_ref, f32[8]{0:T(128)S(1)} %copy-done.3, f32[16]{0:T(128)S(1)} %copy-done.4, s32[8]{0:T(128)S(1)} %copy-done.5, bf16[2,2,16,12,16,128]{5,4,3,2,1,0:T(8,128)(2,1)S(1)} %copy-done, ...), custom_call_target="tpu_custom_call" | custom-call | tf_op jit(solution)/shard_map/panels/pallas_call | solution.py:652
  140.8 8.3 %tile.1 = f32[1500,2,750]{2,1,0:T(2,128)} custom-call(f32[1536,1536]{1,0:T(8,128)S(1)} %get-tuple-element.8.acc_ref, bf16[1536,896]{1,0:T(8,128)(2,1)S(1)} %get-tuple-element.9.left_ref, bf16[896,1536]{1,0:T(8,128)(2,1)S(1)} %get-tuple-element.10.right_ref), custom_call_target="tpu_custom_call" | custom-call | tf_op jit(solution)/shard_map/tile/pallas_call | solution.py:708
Async XLA Ops:
  0.0 76.7 %copy-start.1 = (bf16[512,512]{1,0:T(8,128)(2,1)S(1)}, bf16[512,512]{1,0:T(8,128)(2,1)}, u32[]{:S(2)}) copy-start(bf16[512,512]{1,0:T(8,128)(2,1)} %constant.196.clone.order_ref) | copy-start | bytes 1572868
  0.0 76.7 %copy-start.2 = (bf16[256,512]{1,0:T(8,128)(2,1)S(1)}, bf16[256,512]{1,0:T(8,128)(2,1)}, u32[]{:S(2)}) copy-start(bf16[256,512]{1,0:T(8,128)(2,1)} %constant.195.clone.tab_ref) | copy-start | bytes 786436
  0.0 76.7 %copy-start.5 = (s32[8]{0:T(128)S(1)}, s32[8]{0:T(128)}, u32[]{:S(2)}) copy-start(s32[8]{0:T(128)} %oc_ref.1) | copy-start | bytes 100
  0.0 76.7 %copy-start.4 = (f32[16]{0:T(128)S(1)}, f32[16]{0:T(128)}, u32[]{:S(2)}) copy-start(f32[16]{0:T(128)} %ce_ref.1) | copy-start | bytes 196
  0.0 76.7 %copy-start.3 = (f32[8]{0:T(128)S(1)}, f32[8]{0:T(128)}, u32[]{:S(2)}) copy-start(f32[8]{0:T(128)} %ve_ref.1) | copy-start | bytes 100
  76.7 1.9 %copy-start = (bf16[2,2,16,12,16,128]{5,4,3,2,1,0:T(8,128)(2,1)S(1)}, bf16[2,2,16,12,16,128]{5,4,3,2,1,0:T(8,128)(2,1)}, u32[]{:S(2)}) copy-start(bf16[2,2,16,12,16,128]{5,4,3,2,1,0:T(8,128)(2,1)} %planes.1.in_ref) | copy-start | bytes 9437188

commit v3 on v2

--- a/solution.py
+++ b/solution.py
@@ -608,7 +608,8 @@
 
     arrange(0, 0)
     arrange(0, 1)
-    for k, (land, d, half) in enumerate(arrivals):
+    def take(k):
+        land, d, half = arrivals[k]
         row_wait(land, d, half)
         if k in (0, 2):
             row_hops[4 + k // 2].start()
@@ -617,6 +618,9 @@
         if k in (0, 2):
             col_hops[4 + k // 2].start()
         arrange(d, half)
+
+    for k in (0, 1, 2, 3, 5):
+        take(k)
         if k == 3:
             for n in range(6):
                 side(n, *own_and_near[n], 1).wait_recv()
@@ -630,7 +634,9 @@
                     left_ref[put, 512 + pair * 128 : 640 + pair * 128] = jnp.concatenate(both, 1)
                 return 0
 
-            lax.fori_loop(0, RP // 256, near, 0)
+            lax.fori_loop(0, RP // 512, near, 0)
+            take(4)
+            lax.fori_loop(RP // 512, RP // 256, near, 0)
     for n in range(6, 8):
         side(n, *own_and_near[n], 1).wait_recv()
     for c in range(2):

time: 150 us -> 152 us (1.013)
  Pallas kernels: 146 us -> 149 us
    pallas_call x1, Pallas kernels: 62.1 us -> 64.8 us  [panels_call(): pl.pallas_call(panels_kernel, name='panels', out_shape=(jax.ShapeDtypeStr...]
where the time goes in v3:
time: 152 us
  Pallas kernels  149 us (98%)
  local copies, waits for them, and re-layouts  1.9 us (1%)
    pallas_call x1, Pallas kernels, planes_call(): pl.pallas_call(planes_kernel, name='planes', out_shape=jax.ShapeDtypeStru...  75.6 us
    pallas_call x1, Pallas kernels, panels_call(): pl.pallas_call(panels_kernel, name='panels', out_shape=(jax.ShapeDtypeStr...  64.8 us
    pallas_call x1, Pallas kernels, tile_call(): pl.pallas_call(tile_kernel, name='tile', grid=(RP // rows,), out_shape=ja...  8.25 us

profile of v3, /device:TPU:1, one launch (start us, length us, event | category | flops | bytes accessed | tf_op | source)
XLA Modules:
  0.0 151.7 jit_solution(15318388546130432228)
XLA Ops:
  0.0 0.0 copy-start.1
  0.0 0.0 copy-start.2
  0.0 0.0 copy-start.5
  0.0 0.0 copy-start.4
  0.0 0.0 copy-start.3
  0.0 1.1 fusion.3.idx_ref
  1.1 75.6 %planes.1.in_ref = bf16[2,2,16,12,16,128]{5,4,3,2,1,0:T(8,128)(2,1)} custom-call(bf16[1,8,128,256]{3,2,1,0:T(8,128)(2,1)} %val_ref.1, bf16[16,8,128,256]{3,2,1,0:T(8,128)(2,1)} %con_ref.1, bf16[1024,256]{1,0:T(8,128)(2,1)} %constant.192.clone.wz_ref, bf16[64,128]{1,0:T(8,128)(2,1)} %constant.193.clone.ty_ref, f32[8,128]{1,0:T(8,128)} %constant.194.clone.mask_ref), custom_call_target="tpu_custom_call" | custom-call | tf_op jit(solution)/shard_map/planes/pallas_call | solution.py:340
  76.7 0.0 copy-done.1
  76.7 0.0 copy-done.2
  76.7 0.0 copy-done.5
  76.7 0.0 copy-done.4
  76.7 0.0 copy-done.3
  76.7 0.0 copy-start
  76.7 1.9 %copy-done = bf16[2,2,16,12,16,128]{5,4,3,2,1,0:T(8,128)(2,1)S(1)} copy-done((bf16[2,2,16,12,16,128]{5,4,3,2,1,0:T(8,128)(2,1)S(1)}, bf16[2,2,16,12,16,128]{5,4,3,2,1,0:T(8,128)(2,1)}, u32[]{:S(2)}) %copy-start) | copy-done | bytes 3145752
  78.6 64.8 %panels.1 = (f32[1536,1536]{1,0:T(8,128)S(1)}, bf16[1536,896]{1,0:T(8,128)(2,1)S(1)}, bf16[896,1536]{1,0:T(8,128)(2,1)S(1)}) custom-call(s32[12000]{0:T(1024)S(1)} %fusion.3.idx_ref, f32[8]{0:T(128)S(1)} %copy-done.3, f32[16]{0:T(128)S(1)} %copy-done.4, s32[8]{0:T(128)S(1)} %copy-done.5, bf16[2,2,16,12,16,128]{5,4,3,2,1,0:T(8,128)(2,1)S(1)} %copy-done, ...), custom_call_target="tpu_custom_call" | custom-call | tf_op jit(solution)/shard_map/panels/pallas_call | solution.py:658
  143.4 8.3 %tile.1 = f32[1500,2,750]{2,1,0:T(2,128)} custom-call(f32[1536,1536]{1,0:T(8,128)S(1)} %get-tuple-element.8.acc_ref, bf16[1536,896]{1,0:T(8,128)(2,1)S(1)} %get-tuple-element.9.left_ref, bf16[896,1536]{1,0:T(8,128)(2,1)S(1)} %get-tuple-element.10.right_ref), custom_call_target="tpu_custom_call" | custom-call | tf_op jit(solution)/shard_map/tile/pallas_call | solution.py:714
Async XLA Ops:
  0.0 76.7 %copy-start.1 = (bf16[512,512]{1,0:T(8,128)(2,1)S(1)}, bf16[512,512]{1,0:T(8,128)(2,1)}, u32[]{:S(2)}) copy-start(bf16[512,512]{1,0:T(8,128)(2,1)} %constant.196.clone.order_ref) | copy-start | bytes 1572868
  0.0 76.7 %copy-start.2 = (bf16[256,512]{1,0:T(8,128)(2,1)S(1)}, bf16[256,512]{1,0:T(8,128)(2,1)}, u32[]{:S(2)}) copy-start(bf16[256,512]{1,0:T(8,128)(2,1)} %constant.195.clone.tab_ref) | copy-start | bytes 786436
  0.0 76.7 %copy-start.5 = (s32[8]{0:T(128)S(1)}, s32[8]{0:T(128)}, u32[]{:S(2)}) copy-start(s32[8]{0:T(128)} %oc_ref.1) | copy-start | bytes 100
  0.0 76.7 %copy-start.4 = (f32[16]{0:T(128)S(1)}, f32[16]{0:T(128)}, u32[]{:S(2)}) copy-start(f32[16]{0:T(128)} %ce_ref.1) | copy-start | bytes 196
  0.0 76.7 %copy-start.3 = (f32[8]{0:T(128)S(1)}, f32[8]{0:T(128)}, u32[]{:S(2)}) copy-start(f32[8]{0:T(128)} %ve_ref.1) | copy-start | bytes 100
  76.7 1.9 %copy-start = (bf16[2,2,16,12,16,128]{5,4,3,2,1,0:T(8,128)(2,1)S(1)}, bf16[2,2,16,12,16,128]{5,4,3,2,1,0:T(8,128)(2,1)}, u32[]{:S(2)}) copy-start(bf16[2,2,16,12,16,128]{5,4,3,2,1,0:T(8,128)(2,1)} %planes.1.in_ref) | copy-start | bytes 9437188

commit v4 on v2

--- a/solution.py
+++ b/solution.py
@@ -146,7 +146,7 @@
 
 
 def planes_kernel(
-    val_ref, con_ref, wz_ref, ty_ref, mask_ref, out_ref, val, con, msg, wz, even, odd, first_even, first_odd, scr, con_sem, own_sem, wz_sem, vs, vr, ms, mr, local_sem
+    val_ref, con_ref, wz_ref, ty_ref, mask_ref, tab_ref, xb_ref, out_ref, part, val, con, msg, wz, even, odd, first_even, first_odd, scr, con_sem, own_sem, wz_sem, vs, vr, ms, mr, local_sem
 ):
     g, gat = place_in_groups()
     s, sat = place_in_slabs()
@@ -317,18 +317,36 @@
         pack(vg, half, s)
         kept(vg, half).start()
 
-    def finish(i, _):
-        other = lax.rem(s + i + 1, NSLAB)
+    scaling = 0.5 / float(NF) ** 1.5
+    for vg in range(2):
+        for half in range(2):
+
+            def finish(i, _):
+                arrival(vg, half, lax.rem(s + i + 1, NSLAB)).wait_recv()
+                return 0
+
+            lax.fori_loop(0, NSLAB - 1, finish, 0)
+            kept(vg, half).wait()
+            for p in range(NR // 2):
+                held = out_ref[vg, half, :, p].reshape(2 * NF, 128)
+                both = jnp.dot(tab_ref[:, half * 256 : half * 256 + 256], held, preferred_element_type=F32)
+                for r in range(2):
+                    o = both[r * 128 : r * 128 + 64] + both[r * 128 + 64 : r * 128 + 128]
+                    if half == 0:
+                        part[2 * p + r] = o
+                    else:
+                        o = ((o + part[2 * p + r]) * scaling).astype(BF)
+                        put = (2 * p + r) * KB
+                        xb_ref[put : put + KB, vg * 128 : vg * 128 + 128] = o[0:32]
+                        xb_ref[put : put + KB, 256 + vg * 128 : 384 + vg * 128] = o[32:64]
+
+    def sent(i, _):
         for vg in range(2):
             for half in range(2):
-                arrival(vg, half, other).wait_recv()
-                message(vg, half, other).wait_send()
+                message(vg, half, lax.rem(s + i + 1, NSLAB)).wait_send()
         return 0
 
-    lax.fori_loop(0, NSLAB - 1, finish, 0)
-    for vg in range(2):
-        for half in range(2):
-            kept(vg, half).wait()
+    lax.fori_loop(0, NSLAB - 1, sent, 0)
     for copies in (to_partner, to_ahead, to_behind, p_ahead, p_behind, l_ahead, r_behind):
         for half in range(2):
             copies[half].wait_send()
@@ -340,10 +358,12 @@
     return pl.pallas_call(
         planes_kernel,
         name="planes",
-        out_shape=jax.ShapeDtypeStruct((2, 2, NSLAB, NR // 2, 16, 128), BF),
-        in_specs=[anywhere, anywhere, anywhere, vmem, vmem],
+        out_shape=jax.ShapeDtypeStruct((NBOX, 512), BF),
+        in_specs=[anywhere, anywhere, anywhere, vmem, vmem, vmem],
         out_specs=vmem,
         scratch_shapes=[
+            pltpu.VMEM((2, 2, NSLAB, NR // 2, 16, 128), BF),
+            pltpu.VMEM((NR, 2 * KB, 128), F32),
             pltpu.VMEM((8, NX, NF, 2 * NF), BF),
             pltpu.VMEM((NSLAB, NX, NF, 2 * NF), BF),
             pltpu.VMEM((2, 2, NSLAB, NR // 2, 16, 128), BF),
@@ -371,19 +391,19 @@
         jnp.asarray(depth_weights()),
         jnp.asarray(height_weights()),
         jnp.asarray(wide_mask()),
+        jnp.asarray(box_weights()),
     )
 
 
 def panels_kernel(
-    idx_ref, ve_ref, ce_ref, oc_ref, in_ref, tab_ref, order_ref, acc_ref, left_ref, right_ref,
-    rp_ref, cab_ref, xb, wide, box, blk, rows, cols, landed, cp,
+    idx_ref, ve_ref, ce_ref, oc_ref, xb_ref, order_ref, acc_ref, left_ref, right_ref,
+    rp_ref, cab_ref, wide, box, blk, rows, cols, landed, cp,
     rsa, rra, csa, cra, rs, rr, cs, cr, sib_s, sib_r, lsem,
 ):
     g, gat = place_in_groups()
     s, sat = place_in_slabs()
     gx, gz = g // 2, lax.rem(g, 2)
     sz, yc, sc = s // 8, lax.rem(s, 8), lax.rem(s, 2)
-    scaling = 0.5 / float(NF) ** 1.5
 
     barrier = pltpu.get_barrier_semaphore()
     for i in range(2 * NSLAB):
@@ -394,21 +414,7 @@
         to = {"grp": gat(i // 4, i // 2 % 2), "slab": sat(0, i % 2, 0)}
         pl.semaphore_signal(barrier, inc=1, device_id=to, device_id_type=MESH)
 
-    def four_rows(j, _):
-        for k in range(2):
-            p = j * 2 + k
-            a = [in_ref[vg, :, :, pl.ds(p, 1)].reshape(4 * NF, 128) for vg in range(2)]
-            both = jnp.dot(tab_ref[...], jnp.concatenate(a, 1), preferred_element_type=F32)
-            for r in range(2):
-                o = both[r * 128 : r * 128 + 128]
-                o = ((o[0:64] + o[64:128]) * scaling).astype(BF)
-                put = pl.ds(pl.multiple_of((p * 2 + r) * KB, KB), KB)
-                xb[put, 0:256] = o[0:32]
-                xb[put, 256:512] = o[32:64]
-        return 0
-
-    lax.fori_loop(0, NR // 4, four_rows, 0)
-    wide[...] = jnp.dot(xb[...], order_ref[...], preferred_element_type=F32)
+    wide[...] = jnp.dot(xb_ref[...], order_ref[...], preferred_element_type=F32)
 
     def spread(j, _):
         base = pl.multiple_of(j * 96, 32)
@@ -657,12 +663,11 @@
             jax.ShapeDtypeStruct((RP, 896), BF),
             jax.ShapeDtypeStruct((896, 2 * CP), BF),
         ),
-        in_specs=[smem, smem, smem, smem, vmem, vmem, vmem],
+        in_specs=[smem, smem, smem, smem, vmem, vmem],
         out_specs=(vmem, vmem, vmem),
         scratch_shapes=[
             pltpu.VMEM((4, 2, RP, 256), BF),
             pltpu.VMEM((1536, 2 * CP), BF),
-            pltpu.VMEM((NBOX, 512), BF),
             pltpu.VMEM((NBOX, 512), F32),
             pltpu.VMEM((KB * NBOX, 128), F32),
             pltpu.VMEM((CP + 32, 128), F32),
@@ -691,7 +696,6 @@
         conduction_energy,
         occupation,
         planes,
-        jnp.asarray(box_weights()),
         jnp.asarray(lane_order()),
     )
 

time: 150 us -> 147 us (0.980)
  Pallas kernels: 146 us -> 144 us
    pallas_call x1, Pallas kernels: 62.1 us -> 60.5 us  [panels_call(): pl.pallas_call(panels_kernel, name='panels', out_shape=(jax.ShapeDtypeStr...]
where the time goes in v4:
time: 147 us
  Pallas kernels  144 us (98%)
    pallas_call x1, Pallas kernels, planes_call(): pl.pallas_call(planes_kernel, name='planes', out_shape=jax.ShapeDtypeStru...  75.7 us
    pallas_call x1, Pallas kernels, panels_call(): pl.pallas_call(panels_kernel, name='panels', out_shape=(jax.ShapeDtypeStr...  60.5 us
    pallas_call x1, Pallas kernels, tile_call(): pl.pallas_call(tile_kernel, name='tile', grid=(RP // rows,), out_shape=ja...  8.19 us

profile of v4, /device:TPU:1, one launch (start us, length us, event | category | flops | bytes accessed | tf_op | source)
XLA Modules:
  0.0 146.6 jit_solution(7274951457205574043)
XLA Ops:
  0.0 0.0 copy-start.1
  0.0 0.0 copy-start.4
  0.0 0.0 copy-start.3
  0.0 0.0 copy-start.2
  0.0 1.1 fusion.3.idx_ref
  1.1 75.7 %planes.1.xb_ref = bf16[768,512]{1,0:T(8,128)(2,1)} custom-call(bf16[1,8,128,256]{3,2,1,0:T(8,128)(2,1)} %val_ref.1, bf16[16,8,128,256]{3,2,1,0:T(8,128)(2,1)} %con_ref.1, bf16[1024,256]{1,0:T(8,128)(2,1)} %constant.192.clone.wz_ref, bf16[64,128]{1,0:T(8,128)(2,1)} %constant.193.clone.ty_ref, f32[8,128]{1,0:T(8,128)} %constant.194.clone.mask_ref, ...), custom_call_target="tpu_custom_call" | custom-call | tf_op jit(solution)/shard_map/planes/pallas_call | solution.py:358
  76.8 0.0 copy-done.1
  76.8 0.0 copy-done.4
  76.8 0.0 copy-done.3
  76.8 0.0 copy-done.2
  76.8 0.0 copy-start
  76.8 1.1 copy-done
  78.0 60.5 %panels.1 = (f32[1536,1536]{1,0:T(8,128)S(1)}, bf16[1536,896]{1,0:T(8,128)(2,1)S(1)}, bf16[896,1536]{1,0:T(8,128)(2,1)S(1)}) custom-call(s32[12000]{0:T(1024)S(1)} %fusion.3.idx_ref, f32[8]{0:T(128)S(1)} %copy-done.2, f32[16]{0:T(128)S(1)} %copy-done.3, s32[8]{0:T(128)S(1)} %copy-done.4, bf16[768,512]{1,0:T(8,128)(2,1)S(1)} %copy-done, ...), custom_call_target="tpu_custom_call" | custom-call | tf_op jit(solution)/shard_map/panels/pallas_call | solution.py:658
  138.5 8.2 %tile.1 = f32[1500,2,750]{2,1,0:T(2,128)} custom-call(f32[1536,1536]{1,0:T(8,128)S(1)} %get-tuple-element.8.acc_ref, bf16[1536,896]{1,0:T(8,128)(2,1)S(1)} %get-tuple-element.9.left_ref, bf16[896,1536]{1,0:T(8,128)(2,1)S(1)} %get-tuple-element.10.right_ref), custom_call_target="tpu_custom_call" | custom-call | tf_op jit(solution)/shard_map/tile/pallas_call | solution.py:712
Async XLA Ops:
  0.0 76.8 %copy-start.1 = (bf16[512,512]{1,0:T(8,128)(2,1)S(1)}, bf16[512,512]{1,0:T(8,128)(2,1)}, u32[]{:S(2)}) copy-start(bf16[512,512]{1,0:T(8,128)(2,1)} %constant.196.clone.order_ref) | copy-start | bytes 1572868
  0.0 76.8 %copy-start.4 = (s32[8]{0:T(128)S(1)}, s32[8]{0:T(128)}, u32[]{:S(2)}) copy-start(s32[8]{0:T(128)} %oc_ref.1) | copy-start | bytes 100
  0.0 76.8 %copy-start.3 = (f32[16]{0:T(128)S(1)}, f32[16]{0:T(128)}, u32[]{:S(2)}) copy-start(f32[16]{0:T(128)} %ce_ref.1) | copy-start | bytes 196
  0.0 76.8 %copy-start.2 = (f32[8]{0:T(128)S(1)}, f32[8]{0:T(128)}, u32[]{:S(2)}) copy-start(f32[8]{0:T(128)} %ve_ref.1) | copy-start | bytes 100
  76.8 1.1 copy-start
